TPU v7x, 512 devices: a whole 4x4x16 slice. The times are simulated.
512 devices in a mesh: section: 16 (over y, x), expert: 32 (over z, core).
Axes of the slice: x: 4, y: 4, z: 16, core: 2. Of those that a mesh axis runs over, the one named last changes fastest.
Arguments:
- grad_in: bfloat16 [16, 2, 1024, 3584], P('section', None, 'expert'), may hold values from -6 to 6
- fresh_grad: bfloat16 [2, 1024, 3584], P(None, 'expert'), may hold values from -6 to 6
- routes: int32 [16, 2, 2, 1024, 2], P('section', None, None, 'expert'), may hold values from 0 to 7, all different within a row; in each aligned block of 32 rows (0 to 31, 32 to 63, ..., all dimensions but the last counted through in order) at most 12 rows name the same one
- gate_weights: bfloat16 [16, 2, 2, 1024, 2], P('section', None, None, 'expert'), may hold values from 0.099609375 to 1
- saved_pre: bfloat16 [16, 2, 2, 384, 8192], P('section', None, None, None, 'expert'), may hold values from -6 to 6
- w_up: bfloat16 [16, 3584, 8192], P('section', None, 'expert'), may hold values from -0.1875 to 0.1875
- w_down: bfloat16 [16, 8192, 3584], P('section', 'expert'), may hold values from -0.09375 to 0.09375
Outputs:
- grad_out: bfloat16 [16, 2, 1024, 3584], P('section', None, 'expert')
Inputs may be any that keep to these rules, and one draw needn't show every extreme that they name: `routes`: each token names 2 different experts. Among the 32 tokens of one device no expert is named more than 12 times, and in every draw some device names some expert exactly 12 times.
All inputs are finite; a program needn't handle non-finite values.
Results may differ from a plain program's by a relative error of at most 0.011.
Values may be sent and summed in bfloat16 or wider, within the bound.
No kernel may reach another device: no remote copies, remote signals or barrier semaphores. Data moves between devices by JAX's collectives and lax.ppermute only.
A program may use at most 128 MiB of HBM per device.

v0:
```python
import jax
import jax.numpy as jnp
from jax import lax
from jax.sharding import PartitionSpec as P

SLICES = 4
STEPS = 2


highest = lax.Precision.HIGHEST


def from_behind(block, axis, distance):
    devices = range(lax.axis_size(axis))
    route = [(i - distance, i) for i in devices if i - distance in devices]
    return lax.ppermute(block, axis, route)


def slot_tables(routes, gate_weights, experts, capacity):
    experts_all = jnp.arange(experts, dtype=jnp.int32)
    matches = (routes[..., None] == experts_all).astype(jnp.int32)
    chosen = jnp.sum(matches, axis=-2)
    scaled = jnp.sum(
        matches.astype(jnp.float32) * gate_weights.astype(jnp.float32)[..., None], axis=-2
    )
    ranking = jnp.cumsum(chosen, axis=-2) - chosen
    ranking_t = jnp.swapaxes(ranking, -1, -2)
    chosen_t = jnp.swapaxes(chosen, -1, -2)
    columns = jnp.arange(capacity, dtype=jnp.int32)
    placed = ((ranking_t[..., None, :] == columns[:, None]) & (chosen_t[..., None, :] > 0)).astype(
        jnp.float32
    )
    return (placed, scaled)


def layer(incoming, routes, gate_weights, saved_pre, w_up, w_down):
    batches = incoming.shape[0]
    feat_width = incoming.shape[2]
    groups = lax.axis_size("expert")
    experts = groups // SLICES
    capacity = saved_pre.shape[1] // groups
    placed, scaled = slot_tables(routes, gate_weights, experts, capacity)
    mixing = (placed * jnp.swapaxes(scaled, 1, 2)[:, :, None, :]).astype(jnp.bfloat16)
    outgoing = jnp.einsum(
        "kect,ktd->kecd", mixing, incoming, preferred_element_type=jnp.float32
    ).astype(jnp.bfloat16)
    outgoing = jnp.repeat(outgoing, SLICES, axis=1)
    received = lax.all_to_all(outgoing, "expert", split_axis=1, concat_axis=1, tiled=True)
    slot_rows = received.reshape(batches, groups * capacity, feat_width)
    hidden_grad = jnp.einsum("krd,fd->krf", slot_rows, w_down, preferred_element_type=jnp.float32)
    preact = saved_pre.astype(jnp.float32)
    logistic = jax.nn.sigmoid(preact)
    pre_grad = (hidden_grad * logistic * (1.0 + preact * (1.0 - logistic))).astype(jnp.bfloat16)
    pieces = jnp.einsum("krf,df->krd", pre_grad, w_up, preferred_element_type=jnp.float32).astype(
        jnp.bfloat16
    )
    returned = lax.all_to_all(
        pieces.reshape(batches, groups, capacity, feat_width),
        "expert",
        split_axis=1,
        concat_axis=1,
        tiled=True,
    )
    summed = jnp.sum(
        returned.reshape(batches, experts, SLICES, capacity, feat_width).astype(jnp.float32), axis=2
    )
    routed_sum = jnp.einsum("kect,kecd->ktd", placed, summed, precision=highest)
    return (incoming.astype(jnp.float32) + routed_sum).astype(jnp.bfloat16)


def body(grad_in, fresh_grad, routes, gate_weights, saved_pre, w_up, w_down):
    section_id = lax.axis_index("section")
    sections = lax.axis_size("section")
    current = grad_in[0]
    result = current
    for step_now in range(STEPS):
        result = jnp.concatenate(
            [
                layer(
                    current[lane_index : lane_index + 1],
                    routes[0, step_now, lane_index : lane_index + 1],
                    gate_weights[0, step_now, lane_index : lane_index + 1],
                    saved_pre[0, step_now, lane_index : lane_index + 1],
                    w_up[0],
                    w_down[0],
                )
                for lane_index in range(2)
            ],
            axis=0,
        )
        if step_now + 1 < STEPS:
            from_above = from_behind(result[0], "section", -1)
            from_below = from_behind(result[1], "section", 1)
            toward_lower = jnp.where(section_id == sections - 1, fresh_grad[0], from_above)
            toward_higher = jnp.where(section_id == 0, fresh_grad[1], from_below)
            current = jnp.stack([toward_lower, toward_higher])
    return result[None]


def solution(mesh):
    placed = (
        P("section", None, "expert", None),
        P(None, "expert", None),
        P("section", None, None, "expert", None),
        P("section", None, None, "expert", None),
        P("section", None, None, None, "expert"),
        P("section", None, "expert"),
        P("section", "expert", None),
    )
    return jax.shard_map(
        body,
        mesh=mesh,
        in_specs=placed,
        out_specs=P("section", None, "expert", None),
        check_vma=False,
    )
```

profile of v0, /device:TPU:25, one launch (start us, length us, event | category | flops | bytes accessed | tf_op | source)
XLA Modules:
  0.0 1395.2 jit_solution(8303352586399564034)
XLA Ops:
  5.4 16.1 %all-to-all-start = ((bf16[1,32,12,3584]{3,2,0,1:T(8,128)(2,1)}), bf16[1,32,12,3584]{3,2,0,1:T(8,128)(2,1)}, u32[]{:S(2)}, u32[]{:S(2)}) async-start(bf16[1,32,12,3584]{3,2,0,1:T(8,128)(2,1)} %bitcast.253), calls=%async_computation | async-start | bytes 7340032 | tf_op jit(solution)/shard_map/all_to_all | solution.py:48
  22.3 161.3 %all-to-all-done = bf16[1,32,12,3584]{3,2,0,1:T(8,128)(2,1)} async-done(((bf16[1,32,12,3584]{3,2,0,1:T(8,128)(2,1)}), bf16[1,32,12,3584]{3,2,0,1:T(8,128)(2,1)}, u32[]{:S(2)}, u32[]{:S(2)}) %all-to-all-start) | async-done | bytes 2752544 | tf_op jit(solution)/shard_map/all_to_all | solution.py:48
  185.9 9.3 all-to-all-start.4
  195.2 5.4 reshape.538
  200.7 6.9 convolution_convert_fusion.3
  212.8 144.3 %all-to-all-done.4 = bf16[1,32,12,3584]{3,2,0,1:T(8,128)(2,1)} async-done(((bf16[1,32,12,3584]{3,2,0,1:T(8,128)(2,1)}), bf16[1,32,12,3584]{3,2,0,1:T(8,128)(2,1)}, u32[]{:S(2)}, u32[]{:S(2)}) %all-to-all-start.4) | async-done | bytes 2752544 | tf_op jit(solution)/shard_map/all_to_all | solution.py:48
  357.2 9.3 all-to-all-start.1
  366.5 5.4 reshape.542
  371.9 6.9 convolution_convert_fusion.1
  384.1 144.3 %all-to-all-done.1 = bf16[1,32,12,3584]{3,2,0,1:T(8,128)(2,1)} async-done(((bf16[1,32,12,3584]{3,2,0,1:T(8,128)(2,1)}), bf16[1,32,12,3584]{3,2,0,1:T(8,128)(2,1)}, u32[]{:S(2)}, u32[]{:S(2)}) %all-to-all-start.1) | async-done | bytes 2752544 | tf_op jit(solution)/shard_map/all_to_all | solution.py:57
  528.4 9.3 all-to-all-start.5
  551.3 148.4 %all-to-all-done.5 = bf16[1,32,12,3584]{3,2,0,1:T(8,128)(2,1)} async-done(((bf16[1,32,12,3584]{3,2,0,1:T(8,128)(2,1)}), bf16[1,32,12,3584]{3,2,0,1:T(8,128)(2,1)}, u32[]{:S(2)}, u32[]{:S(2)}) %all-to-all-start.5) | async-done | bytes 2752544 | tf_op jit(solution)/shard_map/all_to_all | solution.py:57
  702.0 9.3 all-to-all-start.2
  718.5 7.6 collective-permute-done.1
  728.1 145.4 %all-to-all-done.2 = bf16[1,32,12,3584]{3,2,0,1:T(8,128)(2,1)} async-done(((bf16[1,32,12,3584]{3,2,0,1:T(8,128)(2,1)}), bf16[1,32,12,3584]{3,2,0,1:T(8,128)(2,1)}, u32[]{:S(2)}, u32[]{:S(2)}) %all-to-all-start.2) | async-done | bytes 2752544 | tf_op jit(solution)/shard_map/all_to_all | solution.py:48
  875.8 9.1 all-to-all-start.6
  884.9 5.4 reshape.540
  890.3 6.9 convolution_convert_fusion.2
  902.6 144.2 %all-to-all-done.6 = bf16[1,32,12,3584]{3,2,0,1:T(8,128)(2,1)} async-done(((bf16[1,32,12,3584]{3,2,0,1:T(8,128)(2,1)}), bf16[1,32,12,3584]{3,2,0,1:T(8,128)(2,1)}, u32[]{:S(2)}, u32[]{:S(2)}) %all-to-all-start.6) | async-done | bytes 2752544 | tf_op jit(solution)/shard_map/all_to_all | solution.py:48
  1046.8 9.3 all-to-all-start.3
  1061.5 6.9 convolution_convert_fusion
  1073.7 144.4 %all-to-all-done.3 = bf16[1,32,12,3584]{3,2,0,1:T(8,128)(2,1)} async-done(((bf16[1,32,12,3584]{3,2,0,1:T(8,128)(2,1)}), bf16[1,32,12,3584]{3,2,0,1:T(8,128)(2,1)}, u32[]{:S(2)}, u32[]{:S(2)}) %all-to-all-start.3) | async-done | bytes 2752544 | tf_op jit(solution)/shard_map/all_to_all | solution.py:57
  1218.1 9.3 all-to-all-start.7
  1231.6 158.2 %all-to-all-done.7 = bf16[1,32,12,3584]{3,2,0,1:T(8,128)(2,1)} async-done(((bf16[1,32,12,3584]{3,2,0,1:T(8,128)(2,1)}), bf16[1,32,12,3584]{3,2,0,1:T(8,128)(2,1)}, u32[]{:S(2)}, u32[]{:S(2)}) %all-to-all-start.7) | async-done | bytes 2752544 | tf_op jit(solution)/shard_map/all_to_all | solution.py:57
  (76 shorter events, 71.6 us)
Async XLA Ops:
  0.0 200.7 %copy-start = (bf16[1,3584,256]{2,1,0:T(8,128)(2,1)S(1)}, bf16[1,3584,256]{2,1,0:T(8,128)(2,1)}, u32[]{:S(2)}) copy-start(bf16[1,3584,256]{2,1,0:T(8,128)(2,1)} %param.12) | copy-start | bytes 5505028
  5.4 16.4 %copy-start.3 = (bf16[1,2,32,3584]{3,2,1,0:T(8,128)(2,1)S(1)}, bf16[1,2,32,3584]{3,2,1,0:T(8,128)(2,1)}, u32[]{:S(2)}) copy-start(bf16[1,2,32,3584]{3,2,1,0:T(8,128)(2,1)} %param.7) | copy-start | bytes 1376260
  5.4 178.1 %all-to-all-start = ((bf16[1,32,12,3584]{3,2,0,1:T(8,128)(2,1)}), bf16[1,32,12,3584]{3,2,0,1:T(8,128)(2,1)}, u32[]{:S(2)}, u32[]{:S(2)}) async-start(bf16[1,32,12,3584]{3,2,0,1:T(8,128)(2,1)} %bitcast.253), calls=%async_computation | async-start | bytes 7340032 | tf_op jit(solution)/shard_map/all_to_all | solution.py:48
  185.9 171.3 %all-to-all-start.4 = ((bf16[1,32,12,3584]{3,2,0,1:T(8,128)(2,1)}), bf16[1,32,12,3584]{3,2,0,1:T(8,128)(2,1)}, u32[]{:S(2)}, u32[]{:S(2)}) async-start(bf16[1,32,12,3584]{3,2,0,1:T(8,128)(2,1)} %bitcast.254), calls=%async_computation.4 | async-start | bytes 7340032 | tf_op jit(solution)/shard_map/all_to_all | solution.py:48
  195.2 5.5 copy-start.8
  357.2 171.3 %all-to-all-start.1 = ((bf16[1,32,12,3584]{3,2,0,1:T(8,128)(2,1)}), bf16[1,32,12,3584]{3,2,0,1:T(8,128)(2,1)}, u32[]{:S(2)}, u32[]{:S(2)}) async-start(bf16[1,32,12,3584]{3,2,0,1:T(8,128)(2,1)} %bitcast.249), calls=%async_computation.1 | async-start | bytes 7340032 | tf_op jit(solution)/shard_map/all_to_all | solution.py:57
  528.4 171.3 %all-to-all-start.5 = ((bf16[1,32,12,3584]{3,2,0,1:T(8,128)(2,1)}), bf16[1,32,12,3584]{3,2,0,1:T(8,128)(2,1)}, u32[]{:S(2)}, u32[]{:S(2)}) async-start(bf16[1,32,12,3584]{3,2,0,1:T(8,128)(2,1)} %bitcast.248), calls=%async_computation.5 | async-start | bytes 7340032 | tf_op jit(solution)/shard_map/all_to_all | solution.py:57
  538.0 2.9 copy-start.4
  538.0 13.0 copy-start.2
  541.7 9.3 collective-permute-start
  702.0 171.5 %all-to-all-start.2 = ((bf16[1,32,12,3584]{3,2,0,1:T(8,128)(2,1)}), bf16[1,32,12,3584]{3,2,0,1:T(8,128)(2,1)}, u32[]{:S(2)}, u32[]{:S(2)}) async-start(bf16[1,32,12,3584]{3,2,0,1:T(8,128)(2,1)} %bitcast.252), calls=%async_computation.2 | async-start | bytes 7340032 | tf_op jit(solution)/shard_map/all_to_all | solution.py:48
  711.6 2.9 copy-start.5
  715.3 10.8 collective-permute-start.1
  726.1 0.7 copy-start.6
  875.8 171.1 %all-to-all-start.6 = ((bf16[1,32,12,3584]{3,2,0,1:T(8,128)(2,1)}), bf16[1,32,12,3584]{3,2,0,1:T(8,128)(2,1)}, u32[]{:S(2)}, u32[]{:S(2)}) async-start(bf16[1,32,12,3584]{3,2,0,1:T(8,128)(2,1)} %bitcast.255), calls=%async_computation.6 | async-start | bytes 7340032 | tf_op jit(solution)/shard_map/all_to_all | solution.py:48
  884.9 5.5 copy-start.9
  1046.8 171.3 %all-to-all-start.3 = ((bf16[1,32,12,3584]{3,2,0,1:T(8,128)(2,1)}), bf16[1,32,12,3584]{3,2,0,1:T(8,128)(2,1)}, u32[]{:S(2)}, u32[]{:S(2)}) async-start(bf16[1,32,12,3584]{3,2,0,1:T(8,128)(2,1)} %bitcast.250), calls=%async_computation.3 | async-start | bytes 7340032 | tf_op jit(solution)/shard_map/all_to_all | solution.py:57
  1218.1 171.7 %all-to-all-start.7 = ((bf16[1,32,12,3584]{3,2,0,1:T(8,128)(2,1)}), bf16[1,32,12,3584]{3,2,0,1:T(8,128)(2,1)}, u32[]{:S(2)}, u32[]{:S(2)}) async-start(bf16[1,32,12,3584]{3,2,0,1:T(8,128)(2,1)} %bitcast.251), calls=%async_computation.7 | async-start | bytes 7340032 | tf_op jit(solution)/shard_map/all_to_all | solution.py:57
  1389.8 3.0 copy-start.1
  1389.8 3.8 copy-start.7
where the time goes:
time: 1400 us
  waiting for transfers between devices  1200 us (86%)
  starting transfers between devices  88.9 us (6%)
  local copies, waits for them, and re-layouts  54.4 us (4%)
  matrix products  34.1 us (2%)
  other arithmetic  14.8 us (1%)
    all_to_all x4, waiting for transfers between devices, layer(): lax.all_to_all(pieces.reshape(batches, groups, capacity, feat_width), 'ex...  595 us
    all_to_all x4, waiting for transfers between devices, layer(): lax.all_to_all(outgoing, 'expert', split_axis=1, concat_axis=1, tiled=True)  595 us
    all_to_all x4, starting transfers between devices, layer(): lax.all_to_all(outgoing, 'expert', split_axis=1, concat_axis=1, tiled=True)  43.9 us
    all_to_all x4, starting transfers between devices, layer(): lax.all_to_all(pieces.reshape(batches, groups, capacity, feat_width), 'ex...  37.3 us
  transfers between devices with their start and end apart: 10, of which 10 were waited for; matrix products, arithmetic and copies ran while one was open for 6% of the time, Pallas kernels for 0%

commit v1 on v0

v1 whole, which is shorter than its diff:
```python
import jax
import jax.numpy as jnp
from jax import lax
from jax.sharding import PartitionSpec as P

SLICES = 4
STEPS = 2
INFO = 128


def from_behind(block, axis, distance):
    devices = range(lax.axis_size(axis))
    route = [(i - distance, i) for i in devices if i - distance in devices]
    return lax.ppermute(block, axis, route)


def info_columns(routes, gate_weights):
    steps, lanes, tokens, top = routes.shape
    both = jnp.concatenate([routes.astype(jnp.bfloat16), gate_weights], axis=-1)
    both = jnp.transpose(both, (1, 2, 0, 3)).reshape(lanes * tokens, steps * 2 * top)
    return jnp.pad(both, ((0, 0), (0, INFO - both.shape[1])))


def token_tables(info, saved_pre, steps, lanes, top):
    groups = lax.axis_size("expert")
    expert = (lax.axis_index("expert") // SLICES).astype(jnp.bfloat16)
    tokens = info.shape[0] // groups // lanes
    capacity = saved_pre.shape[2] // groups
    info = info[:, : steps * 2 * top].reshape(groups, lanes, tokens, steps, 2, top)
    info = jnp.transpose(info, (3, 4, 5, 0, 1, 2))
    named = info[:, 0] == expert
    gates = jnp.sum(jnp.where(named, info[:, 1].astype(jnp.float32), 0.0), axis=1)
    chosen = jnp.any(named, axis=1)
    counts = chosen.astype(jnp.int32)
    slot = jnp.cumsum(counts, axis=-1) - counts
    preact = saved_pre.astype(jnp.float32)
    logistic = jax.nn.sigmoid(preact)
    factor = logistic * (1.0 + preact * (1.0 - logistic))
    factor = factor.reshape(steps, lanes, groups, capacity, -1)
    factor = jnp.transpose(factor, (0, 2, 1, 3, 4))
    placed = jnp.zeros((steps, groups, lanes, tokens, factor.shape[-1]), jnp.float32)
    for c in range(capacity):
        placed = jnp.where((slot == c)[..., None], factor[:, :, :, c : c + 1, :], placed)
    return gates, placed


def body(grad_in, fresh_grad, routes, gate_weights, saved_pre, w_up, w_down):
    section_id = lax.axis_index("section")
    sections = lax.axis_size("section")
    groups = lax.axis_size("expert")
    _, lanes, tokens, width = grad_in.shape
    top = routes.shape[-1]
    current = grad_in[0]
    info = info_columns(routes[0], gate_weights[0])
    for step_now in range(STEPS):
        mine = current.reshape(lanes * tokens, width)
        if step_now == 0:
            gathered = lax.all_gather(
                jnp.concatenate([mine, info], axis=1), "expert", axis=0, tiled=True
            )
            gates, factor = token_tables(gathered[:, width:], saved_pre[0], STEPS, lanes, top)
            gathered = gathered[:, :width]
        else:
            gathered = lax.all_gather(mine, "expert", axis=0, tiled=True)
        routed = (gathered.astype(jnp.float32) * gates[step_now].reshape(-1, 1)).astype(jnp.bfloat16)
        hidden = jnp.einsum("rd,fd->rf", routed, w_down[0], preferred_element_type=jnp.float32)
        pre_grad = (hidden * factor[step_now].reshape(hidden.shape)).astype(jnp.bfloat16)
        partial = jnp.einsum(
            "rf,df->rd", pre_grad, w_up[0], preferred_element_type=jnp.float32
        ).astype(jnp.bfloat16)
        summed = lax.psum_scatter(partial, "expert", scatter_dimension=0, tiled=True)
        result = (mine.astype(jnp.float32) + summed.astype(jnp.float32)).astype(jnp.bfloat16)
        result = result.reshape(lanes, tokens, width)
        if step_now + 1 < STEPS:
            from_above = from_behind(result[0], "section", -1)
            from_below = from_behind(result[1], "section", 1)
            toward_lower = jnp.where(section_id == sections - 1, fresh_grad[0], from_above)
            toward_higher = jnp.where(section_id == 0, fresh_grad[1], from_below)
            current = jnp.stack([toward_lower, toward_higher])
    return result[None]


def solution(mesh):
    placed = (
        P("section", None, "expert", None),
        P(None, "expert", None),
        P("section", None, None, "expert", None),
        P("section", None, None, "expert", None),
        P("section", None, None, None, "expert"),
        P("section", None, "expert"),
        P("section", "expert", None),
    )
    return jax.shard_map(
        body,
        mesh=mesh,
        in_specs=placed,
        out_specs=P("section", None, "expert", None),
        check_vma=False,
    )
```

time: 1400 us -> 549 us (0.39)
  waiting for transfers between devices: 1200 us -> 454 us
  starting transfers between devices: 88.9 us -> 6.82 us
  local copies, waits for them, and re-layouts: 54.4 us -> 11.3 us
    all_to_all x8 -> x0, waiting for transfers between devices: 1190 us -> none  [the longest x4 595 us: layer(): lax.all_to_all(pieces.reshape(batches, groups, capacity, feat_width), 'ex...]
    reduce_scatter x0 -> x2, waiting for transfers between devices: none -> 252 us  [body(): lax.psum_scatter(partial, 'expert', scatter_dimension=0, tiled=True)]
    all_gather x0 -> x2, waiting for transfers between devices: none -> 194 us  [the longest x1 97.5 us: body(): lax.all_gather(jnp.concatenate([mine, info], axis=1), 'expert', axis=0, t...]
    all_to_all x8 -> x0, starting transfers between devices: 81.2 us -> none  [the longest x4 43.9 us: layer(): lax.all_to_all(outgoing, 'expert', split_axis=1, concat_axis=1, tiled=True)]
    another operation x4 -> x0, local copies, waits for them, and re-layouts: 21.7 us -> none
    reshape x4 -> x3, local copies, waits for them, and re-layouts: 21.2 us -> 1.11 us  [the longest x1 0.92 us: token_tables(): info[:, :steps * 2 * top].reshape(groups, lanes, tokens, steps, 2, top)]
    dot_general x12 -> x2, matrix products: 34.1 us -> 42.9 us  [body(): jnp.einsum('rf,df->rd', pre_grad, w_up[0], preferred_element_type=jnp.flo...]
  transfers between devices with their start and end apart: 10 -> 6, of which waited for: 10 -> 6; matrix products, arithmetic and copies ran while one was open for 6% -> 1% of each run, Pallas kernels for 0% -> 0%
where the time goes in v1:
time: 549 us; the launch traced here: 545 us
  waiting for transfers between devices  454 us (83%)
  matrix products  42.9 us (8%)
  other arithmetic  16.9 us (3%)
  between operations  13.4 us (2%)
  local copies, waits for them, and re-layouts  11.3 us (2%)
  starting transfers between devices  6.82 us (1%)
    reduce_scatter x2, waiting for transfers between devices, body(): lax.psum_scatter(partial, 'expert', scatter_dimension=0, tiled=True)  252 us
    all_gather x1, waiting for transfers between devices, body(): lax.all_gather(jnp.concatenate([mine, info], axis=1), 'expert', axis=0, t...  97.5 us
    all_gather x1, waiting for transfers between devices, body(): gathered = lax.all_gather(mine, 'expert', axis=0, tiled=True)  96.8 us
    dot_general x2, matrix products, body(): jnp.einsum('rf,df->rd', pre_grad, w_up[0], preferred_element_type=jnp.flo...  42.9 us
  transfers between devices with their start and end apart: 6, of which 6 were waited for; matrix products, arithmetic and copies ran while one was open for 1% of the time, Pallas kernels for 0%

profile of v1, /device:TPU:25, one launch (start us, length us, event | category | flops | bytes accessed | tf_op | source)
XLA Modules:
  0.0 544.9 jit_solution(1458308118242513850)
XLA Ops:
  6.5 0.8 convert_bitcast_fusion
  8.3 1.8 fusion.16
  10.2 1.9 copy.71
  14.0 0.8 copy.80
  15.6 0.8 copy.76
  16.3 97.5 %all-gather.3.cloned.1.call-done = bf16[2048,3712]{1,0:T(8,128)(2,1)} async-done(((bf16[64,3712]{1,0:T(8,128)(2,1)}), bf16[2048,3712]{1,0:T(8,128)(2,1)}) %all-gather.3.cloned.1.call-update) | async-done | bytes 15204368 | tf_op jit(solution)/shard_map/all_gather | solution.py:58
  113.8 1.1 slice.101
  114.8 0.8 copy.68
  115.6 0.9 reshape.89
  117.0 0.8 reduce_window_sum.11
  118.5 7.8 %select_select_fusion = f32[2,32,2,32,256]{4,3,2,1,0:T(8,128)S(1)} fusion(f32[2,32,2,256]{3,2,1,0:T(2,128)S(1)} %copy.96, f32[2,32,2,256]{3,2,1,0:T(2,128)S(1)} %copy.94, f32[2,32,2,256]{3,2,1,0:T(2,128)S(1)} %copy.92, f32[2,32,2,256]{3,2,1,0:T(2,128)S(1)} %copy.90, f32[2,32,2,256]{3,2,1,0:T(2,128)S(1)} %copy.88, f32[2,32,2,256]{3,2,1,0:T(2,128)S(1)} %copy.86, ...), kind=kLoop, calls=%fused_computation.9 | loop fusion | flops 12582912 | bytes 5816320 | tf_op jit(solution)/shard_map/jit(_where)/select_n | solution.py:43
  126.2 2.3 fusion.22
  128.5 21.4 %convolution_convert_fusion.1 = bf16[2048,3584]{1,0:T(8,128)(2,1)} fusion(f32[2048,256]{1,0:T(8,128)} %bitcast.71, bf16[2048,3712]{1,0:T(8,128)(2,1)} %all-gather.3.cloned.1.call-done, f32[2048]{0:T(1024)S(1)} %mul.34, bf16[1,3584,256]{2,1,0:T(8,128)(2,1)S(1)} %copy-done, bf16[1,256,3584]{2,1,0:T(8,128)(2,1)} %param.13), kind=kOutput, calls=%fused_computation.3 | convolution fusion | flops 7546601472 | bytes 35135488 | tf_op jit(solution)/shard_map/rf,df->rd/dot_general | solution.py:68
  150.0 126.2 %reduce-scatter.3.cloned.1.call-done = bf16[64,3584]{1,0:T(8,128)(2,1)} async-done(((bf16[2048,3584]{1,0:T(8,128)(2,1)}), bf16[64,3584]{1,0:T(8,128)(2,1)}) %reduce-scatter.3.cloned.1.call-update) | async-done | bytes 458768 | tf_op jit(solution)/shard_map/reduce_scatter | solution.py:71
  276.2 1.1 add_convert_fusion.1
  277.4 4.6 collective-permute-start
  282.0 2.1 collective-permute-start.1
  284.1 0.8 collective-permute-done
  284.9 5.9 %collective-permute-done.1 = bf16[32,3584]{1,0:T(8,128)(2,1)S(1)} collective-permute-done((bf16[32,3584]{1,0:T(8,128)(2,1)S(1)}, bf16[32,3584]{1,0:T(8,128)(2,1)S(1)}, u32[]{:S(2)}, u32[]{:S(2)}) %collective-permute-start.1) | collective-permute-done | bytes 229408 | tf_op jit(solution)/shard_map/ppermute | solution.py:14
  290.9 0.8 pad_maximum_fusion
  291.9 96.8 %all-gather.5.cloned.1.call-done = bf16[2048,3584]{1,0:T(8,128)(2,1)} async-done(((bf16[64,3584]{1,0:T(8,128)(2,1)}), bf16[2048,3584]{1,0:T(8,128)(2,1)}) %all-gather.5.cloned.1.call-update) | async-done | bytes 14680080 | tf_op jit(solution)/shard_map/all_gather | solution.py:64
  388.7 21.5 %convolution_convert_fusion = bf16[2048,3584]{1,0:T(8,128)(2,1)} fusion(f32[2048,256]{1,0:T(8,128)} %bitcast.70, bf16[2048,3584]{1,0:T(8,128)(2,1)} %all-gather.5.cloned.1.call-done, f32[2048]{0:T(1024)S(1)} %mul.40, bf16[1,3584,256]{2,1,0:T(8,128)(2,1)S(1)} %copy-done, bf16[1,256,3584]{2,1,0:T(8,128)(2,1)} %param.13), kind=kOutput, calls=%fused_computation.2 | convolution fusion | flops 7546601472 | bytes 35135488 | tf_op jit(solution)/shard_map/rf,df->rd/dot_general | solution.py:68
  410.2 126.3 %reduce-scatter.5.cloned.1.call-done = bf16[64,3584]{1,0:T(8,128)(2,1)} async-done(((bf16[2048,3584]{1,0:T(8,128)(2,1)}), bf16[64,3584]{1,0:T(8,128)(2,1)}) %reduce-scatter.5.cloned.1.call-update) | async-done | bytes 458768 | tf_op jit(solution)/shard_map/reduce_scatter | solution.py:71
  536.5 1.9 add_convert_fusion
  (54 shorter events, 4.8 us)
Async XLA Ops:
  6.5 122.0 %copy-start = (bf16[1,3584,256]{2,1,0:T(8,128)(2,1)S(1)}, bf16[1,3584,256]{2,1,0:T(8,128)(2,1)}, u32[]{:S(2)}) copy-start(bf16[1,3584,256]{2,1,0:T(8,128)(2,1)} %param.12) | copy-start | bytes 5505028
  6.5 107.2 %all-gather.3.cloned.1.call-start = ((), (), s32[]{:S(2)}) async-start(), calls=%async_computation.2 | async-start | bytes 15679488 | tf_op jit(solution)/shard_map/all_gather | solution.py:58
  10.1 266.1 %reduce-scatter.3.cloned.1.call-start = ((), (), s32[]{:S(2)}) async-start(), calls=%async_computation.3 | async-start | bytes 15138816 | tf_op jit(solution)/shard_map/reduce_scatter | solution.py:71
  150.0 126.2 %copy-start.2 = (bf16[1,2,32,3584]{3,2,1,0:T(8,128)(2,1)S(1)}, bf16[1,2,32,3584]{3,2,1,0:T(8,128)(2,1)}, u32[]{:S(2)}) copy-start(bf16[1,2,32,3584]{3,2,1,0:T(8,128)(2,1)} %param.7) | copy-start | bytes 1376260
  150.0 140.9 %copy-start.3 = (bf16[2,32,3584]{2,1,0:T(8,128)(2,1)S(1)}, bf16[2,32,3584]{2,1,0:T(8,128)(2,1)}, u32[]{:S(2)}) copy-start(bf16[2,32,3584]{2,1,0:T(8,128)(2,1)} %param.8) | copy-start | bytes 1376260
  150.0 238.7 %all-gather.5.cloned.1.call-start = ((), (), s32[]{:S(2)}) async-start(), calls=%async_computation.4 | async-start | bytes 15138816 | tf_op jit(solution)/shard_map/all_gather | solution.py:64
  277.4 7.5 %collective-permute-start = (bf16[32,3584]{1,0:T(8,128)(2,1)S(1)}, bf16[32,3584]{1,0:T(8,128)(2,1)S(1)}, u32[]{:S(2)}, u32[]{:S(2)}) collective-permute-start(bf16[32,3584]{1,0:T(8,128)(2,1)S(1)} %get-tuple-element.23), channel_id=1, source_target_pairs={{32,0},{64,32},{96,64},{128,96},{160,128},{192,160},{224,192},{256... | collective-permute-start | bytes 688136 | tf_op jit(solution)/shard_map/ppermute | solution.py:14
  282.0 8.9 %collective-permute-start.1 = (bf16[32,3584]{1,0:T(8,128)(2,1)S(1)}, bf16[32,3584]{1,0:T(8,128)(2,1)S(1)}, u32[]{:S(2)}, u32[]{:S(2)}) collective-permute-start(bf16[32,3584]{1,0:T(8,128)(2,1)S(1)} %get-tuple-element.24), channel_id=1, source_target_pairs={{0,32},{32,64},{64,96},{96,128},{128,160},{160,192},{192,224},{224... | collective-permute-start | bytes 688136 | tf_op jit(solution)/shard_map/ppermute | solution.py:14
  291.7 244.7 %reduce-scatter.5.cloned.1.call-start = ((), (), s32[]{:S(2)}) async-start(), calls=%async_computation.5 | async-start | bytes 15138816 | tf_op jit(solution)/shard_map/reduce_scatter | solution.py:71
  410.2 126.3 %copy-start.1 = (bf16[2,32,3584]{2,1,0:T(8,128)(2,1)S(1)}, bf16[2,32,3584]{2,1,0:T(8,128)(2,1)}, u32[]{:S(2)}) copy-start(bf16[2,32,3584]{2,1,0:T(8,128)(2,1)} %pad_maximum_fusion) | copy-start | bytes 1376260
Sparse Core Ops, SparseCore 0:
  10.2 103.4 all-gather.2
  150.1 126.0 reduce-scatter.2
  291.9 96.7 all-gather.4
  410.3 126.1 reduce-scatter.4
